TPU v7x, 32 devices: a whole 2x2x4 slice. The times are simulated.
32 devices in a mesh: groups: 2 (over x), sec: 16 (over z, y, core).
Axes of the slice: x: 2, y: 2, z: 4, core: 2. Of those that a mesh axis runs over, the one named last changes fastest.
Arguments:
- hidden_rows: bfloat16 [128, 7168], P(('groups', 'sec')), parts along dimension 0, may hold values from -6 to 6
- residual: bfloat16 [128, 7168], P(('groups', 'sec')), parts along dimension 0, may hold values from -2 to 2
- expert_ids: int32 [128, 3], P(('groups', 'sec')), parts along dimension 0, may hold values from 0 to 7, all different within a row; in each aligned block of 4 rows (0 to 3, 4 to 7, ...) at most 2 rows name the same one
- router_logits: float32 [128, 3], P(('groups', 'sec')), parts along dimension 0, may hold values from -6 to 6
- w_gate: bfloat16 [7168, 32768], P(None, 'sec'), may hold values from -0.0625 to 0.0625
- w_up: bfloat16 [7168, 32768], P(None, 'sec'), may hold values from -0.0625 to 0.0625
- w_down: bfloat16 [32768, 7168], P('sec'), may hold values from -0.09375 to 0.09375
- queries: bfloat16 [256, 16384], P(('groups', 'sec')), parts along dimension 0, may hold values from -200 to 200
- new_kv: bfloat16 [256, 512], P(('groups', 'sec')), parts along dimension 0, may hold values from -6 to 6
- kv_cache: bfloat16 [256, 64, 512], P(('groups', 'sec')), parts along dimension 0, may hold values from -6 to 6
- cache_slot: int32 [32, 8], P(('groups', 'sec')), parts along dimension 0, may hold values from 0 to 7, each once within a row
- cache_lengths: int32 [256], P(('groups', 'sec')), parts along dimension 0, may hold values from 1 to 64, as said below
Outputs:
- mixed: bfloat16 [128, 7168], P(('groups', 'sec')), parts along dimension 0
- attended: bfloat16 [256, 16384], P(('groups', 'sec')), parts along dimension 0
There are 2 independent parts, one for each index of `groups`. A program takes and returns all parts, laid end to end along the dimension named above; an argument that names none is the same for every part. Nothing has to cross between parts.
Inputs may be any that keep to these rules, and one draw needn't show every extreme that they name: `expert_ids`: in the rows of one device no expert is named more than 2 times; each row names 3 different experts. `cache_lengths`: some request has all 64 positions cached. `cache_slot`: each device's row is an ordering of its 8 slots.
All inputs are finite; a program needn't handle non-finite values.
Results may differ from a plain program's by a relative error of at most 0.0057.
Values may be sent and summed in bfloat16 or wider, within the bound.
A program may use at most 192 MiB of HBM per device.

v0:
```python
import math

import jax
import jax.numpy as jnp
from jax import lax
from jax.sharding import PartitionSpec as P

EXPERTS = 8
TOP = 3
CAP = 2


NEG_FILL = -1e30


def slot_codes(expert_ids, capacity):
    flattened = expert_ids.reshape(-1)
    onehot = (flattened[:, None] == jnp.arange(EXPERTS, dtype=jnp.int32)[None, :]).astype(jnp.int32)
    earlier = jnp.cumsum(onehot, axis=0) - onehot
    position = jnp.sum(earlier * onehot, axis=1)
    return (flattened * capacity + position).reshape(expert_ids.shape)


def per_device(
    hidden_rows,
    residual,
    expert_ids,
    router_logits,
    w_gate,
    w_up,
    w_down,
    queries,
    new_kv,
    kv_cache,
    cache_slot,
    cache_lengths,
):
    devices = lax.axis_size("sec")
    shards = devices // EXPERTS
    tokens_here = hidden_rows.shape[0]
    model_width = hidden_rows.shape[1]
    capacity = CAP
    columns = EXPERTS * capacity
    coded = slot_codes(expert_ids, capacity)
    raised = jax.nn.sigmoid(router_logits)
    gate_weight = raised / jnp.sum(raised, axis=1, keepdims=True)
    picked = coded[:, :, None] == jnp.arange(columns, dtype=jnp.int32)[None, None, :]
    select = jnp.sum(picked, axis=1).astype(jnp.bfloat16)
    packed = jnp.einsum(
        "tc,td->cd", select, hidden_rows, preferred_element_type=jnp.float32
    ).astype(jnp.bfloat16)
    outgoing = jnp.broadcast_to(
        packed.reshape(EXPERTS, 1, capacity, model_width), (EXPERTS, shards, capacity, model_width)
    )
    outgoing = outgoing.reshape(devices, capacity, model_width)
    arrived = lax.all_to_all(outgoing, "sec", split_axis=0, concat_axis=0, tiled=True)
    items = arrived.shape[1]
    flattened = arrived.reshape(-1, model_width)
    gate_proj = jnp.dot(flattened, w_gate, preferred_element_type=jnp.float32)
    up_proj = jnp.dot(flattened, w_up, preferred_element_type=jnp.float32)
    activated = (jax.nn.silu(gate_proj) * up_proj).astype(jnp.bfloat16)
    partial_value = jnp.dot(activated, w_down, preferred_element_type=jnp.float32).astype(
        jnp.bfloat16
    )
    partial_value = partial_value.reshape(devices, items, model_width)
    returned = lax.all_to_all(partial_value, "sec", split_axis=0, concat_axis=0, tiled=True)
    gathered = jnp.sum(
        returned.astype(jnp.float32).reshape(EXPERTS, shards, capacity, model_width), axis=1
    ).reshape(columns, model_width)
    chosen_rows = gathered[coded.reshape(-1)].reshape(tokens_here, TOP, model_width)
    mixed = (
        residual.astype(jnp.float32) + jnp.sum(gate_weight[:, :, None] * chosen_rows, axis=1)
    ).astype(jnp.bfloat16)
    requests_here = queries.shape[0]
    head_size = new_kv.shape[1] // 2
    head_count = queries.shape[1] // head_size
    positions = kv_cache.shape[1]
    cache_rows = kv_cache[cache_slot.reshape(-1)]
    cache_keys = cache_rows[:, :, :head_size]
    cache_values = cache_rows[:, :, head_size:]
    query_heads = queries.reshape(requests_here, head_count, head_size)
    inverse_root = 1.0 / math.sqrt(head_size)
    scores = (
        jnp.einsum("rhd,rcd->rhc", query_heads, cache_keys, preferred_element_type=jnp.float32)
        * inverse_root
    )
    own_score = (
        jnp.einsum(
            "rhd,rd->rh", query_heads, new_kv[:, :head_size], preferred_element_type=jnp.float32
        )
        * inverse_root
    )
    visible = jnp.arange(positions, dtype=jnp.int32)[None, None, :] < cache_lengths[:, None, None]
    scores = jnp.where(visible, scores, NEG_FILL)
    row_max = jnp.maximum(jnp.max(scores, axis=2), own_score)
    lifted = jnp.where(visible, jnp.exp(scores - row_max[:, :, None]), 0.0)
    own_lift = jnp.exp(own_score - row_max)
    denominator = jnp.sum(lifted, axis=2) + own_lift
    weights_bf = (lifted / denominator[:, :, None]).astype(jnp.bfloat16)
    own_bf = (own_lift / denominator).astype(jnp.bfloat16)
    combined = jnp.einsum(
        "rhc,rcd->rhd", weights_bf, cache_values, preferred_element_type=jnp.float32
    )
    combined = (
        combined
        + own_bf.astype(jnp.float32)[:, :, None]
        * new_kv[:, head_size:].astype(jnp.float32)[:, None, :]
    )
    attended = combined.astype(jnp.bfloat16).reshape(requests_here, head_count * head_size)
    return (mixed, attended)


def solution(mesh):
    placed = (
        P(("groups", "sec"), None),
        P(("groups", "sec"), None),
        P(("groups", "sec"), None),
        P(("groups", "sec"), None),
        P(None, "sec"),
        P(None, "sec"),
        P("sec", None),
        P(("groups", "sec"), None),
        P(("groups", "sec"), None),
        P(("groups", "sec"), None, None),
        P(("groups", "sec"), None),
        P(("groups", "sec")),
    )
    return jax.shard_map(
        per_device,
        mesh=mesh,
        in_specs=placed,
        out_specs=(P(("groups", "sec"), None), P(("groups", "sec"), None)),
        check_vma=False,
    )
```

profile of v0, /device:TPU:0, one launch (start us, length us, event | category | flops | bytes accessed | tf_op | source)
XLA Modules:
  0.0 79.3 jit_solution(14802708242152494203)
XLA Ops:
  0.6 0.8 %eq.28 = s32[12]{0:T(128)S(1)} reshape(s32[4,3]{1,0:T(4,128)} %param.14) | data formatting | bytes 96 | tf_op jit(solution)/shard_map/eq | solution.py:18
  1.5 0.2 reduce_window_sum.11
  1.7 0.1 reduce_sum.60
  1.7 0.7 broadcast_multiply_fusion
  2.4 0.1 copy.18
  2.6 1.1 %convolution_convert_fusion.1 = bf16[16,7168]{1,0:T(8,128)(2,1)S(1)} fusion(bf16[4,7168]{1,0:T(4,128)(2,1)} %param.12, s32[4,16]{1,0:T(4,128)S(1)} %convert_reduce_fusion.1), kind=kOutput, calls=%fused_computation.3 | convolution fusion | flops 1032256 | bytes 286976 | tf_op jit(solution)/shard_map/tc,td->cd/dot_general | solution.py:49
  3.7 0.1 broadcast_in_dim.39
  3.8 1.0 %broadcast_in_dim.40 = bf16[8,2,2,7168]{3,2,1,0:T(2,128)(2,1)} broadcast(bf16[8,2,7168]{2,1,0:T(2,128)(2,1)S(1)} %broadcast_in_dim.39), dimensions={0,2,3} | broadcast | bytes 688128 | tf_op jit(solution)/shard_map/broadcast_in_dim | solution.py:52
  4.8 7.4 %all-to-all-start = ((bf16[16,2,7168]{2,1,0:T(2,128)(2,1)}), bf16[16,2,7168]{2,1,0:T(2,128)(2,1)S(1)}, u32[]{:S(2)}, u32[]{:S(2)}) async-start(bf16[16,2,7168]{2,1,0:T(2,128)(2,1)} %bitcast), calls=%async_computation | async-start | bytes 917504 | tf_op jit(solution)/shard_map/all_to_all | solution.py:56
  12.2 0.7 fusion.27
  12.9 0.7 slice_bitcast_fusion
  13.6 0.7 iota_compare_fusion.1
  14.3 0.6 gather_fusion.1
  14.9 1.1 %fusion.12 = f32[8,1,64]{2,1,0:T(1,128)S(1)} fusion(bf16[8,64,256]{2,0,1:T(8,128)(2,1)} %bitcast.33, bf16[8,256,1]{1,0,2:T(8,128)(2,1)S(1)} %get-tuple-element.4), kind=kOutput, calls=%fused_computation.23 | convolution fusion | flops 262144 | bytes 268288 | tf_op jit(solution)/shard_map/rhd,rd->rh/dot_general | solution.py:88
  16.0 1.2 %fusion.31 = (f32[8,64]{1,0:T(8,128)S(1)}, f32[8,64,64]{1,2,0:T(8,128)S(1)}) fusion(bf16[8,64,256]{2,0,1:T(8,128)(2,1)} %bitcast.34, bf16[8,64,512]{2,1,0:T(8,128)(2,1)S(1)} %gather_fusion.1, pred[8,64]{1,0:T(8,128)(4,1)S(1)} %iota_compare_fusion.1), kind=kOutput, calls=%fused_computation.62 | convolution fusion | flops 16875008 | bytes 658432 | tf_op jit(solution)/shard_map/rhd,rcd->rhc/dot_general | solution.py:84
  17.2 0.1 fusion.15
  17.4 8.1 %all-to-all-done = bf16[16,2,7168]{2,1,0:T(2,128)(2,1)S(1)} async-done(((bf16[16,2,7168]{2,1,0:T(2,128)(2,1)}), bf16[16,2,7168]{2,1,0:T(2,128)(2,1)S(1)}, u32[]{:S(2)}, u32[]{:S(2)}) %all-to-all-start) | async-done | bytes 458784 | tf_op jit(solution)/shard_map/all_to_all | solution.py:56
  25.4 0.2 reshape.128
  25.6 12.0 %fusion.32 = f32[32,2048]{1,0:T(8,128)S(1)} fusion(bf16[32,7168]{1,0:T(8,128)(2,1)S(1)} %reshape.128, bf16[7168,2048]{1,0:T(8,128)(2,1)} %param.16), kind=kOutput, calls=%fused_computation.63 | convolution fusion | flops 939524096 | bytes 30081024 | tf_op jit(solution)/shard_map/dot_general | solution.py:59
  37.6 20.8 %convolution_convert_fusion = bf16[32,7168]{1,0:T(8,128)(2,1)S(1)} fusion(bf16[2048,7168]{1,0:T(8,128)(2,1)} %param.18, bf16[32,7168]{1,0:T(8,128)(2,1)S(1)} %reshape.128, bf16[7168,2048]{1,0:T(8,128)(2,1)} %param.17, f32[32,2048]{1,0:T(8,128)S(1)} %fusion.32), kind=kOutput, calls=%fused_computation.2 | convolution fusion | flops 1879670784 | bytes 59899904 | tf_op jit(solution)/shard_map/dot_general | solution.py:62
  58.4 0.9 %reshape.129 = bf16[16,2,7168]{2,1,0:T(2,128)(2,1)} reshape(bf16[32,7168]{1,0:T(8,128)(2,1)S(1)} %convolution_convert_fusion) | data formatting | bytes 917504 | tf_op jit(solution)/shard_map/reshape | solution.py:65
  59.4 3.9 %all-to-all-start.1 = ((bf16[16,2,7168]{2,1,0:T(2,128)(2,1)}), bf16[16,2,7168]{2,1,0:T(2,128)(2,1)S(1)}, u32[]{:S(2)}, u32[]{:S(2)}) async-start(bf16[16,2,7168]{2,1,0:T(2,128)(2,1)} %reshape.129), calls=%async_computation.1 | async-start | bytes 917504 | tf_op jit(solution)/shard_map/all_to_all | solution.py:66
  63.4 0.5 fusion.2
  63.9 0.9 %copy.24 = bf16[1,8,64,256]{3,1,2,0:T(8,128)(2,1)} copy(bf16[1,8,64,256]{3,2,1,0:T(8,128)(2,1)S(1)} %fusion.2) | data formatting | bytes 524288
  64.7 0.1 divide_reduce_fusion
  64.9 11.6 %all-to-all-done.1 = bf16[16,2,7168]{2,1,0:T(2,128)(2,1)S(1)} async-done(((bf16[16,2,7168]{2,1,0:T(2,128)(2,1)}), bf16[16,2,7168]{2,1,0:T(2,128)(2,1)S(1)}, u32[]{:S(2)}, u32[]{:S(2)}) %all-to-all-start.1) | async-done | bytes 458784 | tf_op jit(solution)/shard_map/all_to_all | solution.py:66
  76.5 0.5 convert_reduce_fusion
  77.1 0.3 reshape.132
  77.4 0.7 gather_fusion
  78.1 0.2 reshape.133
  78.2 0.4 multiply_reduce_fusion
  78.6 0.7 add_convert_fusion
  (16 shorter events, 0.3 us)
Async XLA Ops:
  0.6 13.7 %copy-start = (bf16[8,64,512]{2,1,0:T(8,128)(2,1)S(1)}, bf16[8,64,512]{2,1,0:T(8,128)(2,1)}, u32[]{:S(2)}) copy-start(bf16[8,64,512]{2,1,0:T(8,128)(2,1)} %param.21) | copy-start | bytes 1572868
  4.8 20.6 %all-to-all-start = ((bf16[16,2,7168]{2,1,0:T(2,128)(2,1)}), bf16[16,2,7168]{2,1,0:T(2,128)(2,1)S(1)}, u32[]{:S(2)}, u32[]{:S(2)}) async-start(bf16[16,2,7168]{2,1,0:T(2,128)(2,1)} %bitcast), calls=%async_computation | async-start | bytes 917504 | tf_op jit(solution)/shard_map/all_to_all | solution.py:56
  37.6 27.1 %copy-start.2 = (f32[4,3]{1,0:T(4,128)S(1)}, f32[4,3]{1,0:T(4,128)}, u32[]{:S(2)}) copy-start(f32[4,3]{1,0:T(4,128)} %param.15) | copy-start | bytes 148
  37.6 41.0 %copy-start.1 = (bf16[4,7168]{1,0:T(4,128)(2,1)S(1)}, bf16[4,7168]{1,0:T(4,128)(2,1)}, u32[]{:S(2)}) copy-start(bf16[4,7168]{1,0:T(4,128)(2,1)} %param.13) | copy-start | bytes 172036
  59.4 17.2 %all-to-all-start.1 = ((bf16[16,2,7168]{2,1,0:T(2,128)(2,1)}), bf16[16,2,7168]{2,1,0:T(2,128)(2,1)S(1)}, u32[]{:S(2)}, u32[]{:S(2)}) async-start(bf16[16,2,7168]{2,1,0:T(2,128)(2,1)} %reshape.129), calls=%async_computation.1 | async-start | bytes 917504 | tf_op jit(solution)/shard_map/all_to_all | solution.py:66
where the time goes:
time: 79.8 us; the launch traced here: 79.3 us
  matrix products  36.6 us (46%)
  waiting for transfers between devices  19.7 us (25%)
  starting transfers between devices  11.3 us (14%)
  local copies, waits for them, and re-layouts  5.89 us (7%)
  other arithmetic  4.97 us (6%)
    dot_general x1, matrix products, per_device(): jnp.dot(activated, w_down, preferred_element_type=jnp.float32)  20.8 us
    dot_general x1, matrix products, per_device(): gate_proj = jnp.dot(flattened, w_gate, preferred_element_type=jnp.float32)  12 us
    all_to_all x1, waiting for transfers between devices, per_device(): lax.all_to_all(partial_value, 'sec', split_axis=0, concat_axis=0, tiled=T...  11.6 us
    all_to_all x1, waiting for transfers between devices, per_device(): lax.all_to_all(outgoing, 'sec', split_axis=0, concat_axis=0, tiled=True)  8.07 us
    all_to_all x1, starting transfers between devices, per_device(): lax.all_to_all(outgoing, 'sec', split_axis=0, concat_axis=0, tiled=True)  7.39 us
    all_to_all x1, starting transfers between devices, per_device(): lax.all_to_all(partial_value, 'sec', split_axis=0, concat_axis=0, tiled=T...  3.89 us
  transfers between devices with their start and end apart: 2, of which 2 were waited for; matrix products, arithmetic and copies ran while one was open for 9% of the time, Pallas kernels for 0%

commit v1 on v0

--- a/solution.py
+++ b/solution.py
@@ -1,16 +1,506 @@
+import functools
 import math
 
 import jax
 import jax.numpy as jnp
 from jax import lax
+from jax.experimental import pallas as pl
+from jax.experimental.pallas import tpu as pltpu
 from jax.sharding import PartitionSpec as P
 
 EXPERTS = 8
 TOP = 3
 CAP = 2
 
-
 NEG_FILL = -1e30
+
+LANES = 128
+SUB = 8
+BLOCK = SUB * LANES
+VMEM_BYTES = 63 * 1024 * 1024
+SLOTS = 28
+HEADS_STEP = 16
+MESH = pl.DeviceIdType.MESH
+
+
+def iota(shape, dim):
+    return lax.broadcasted_iota(jnp.int32, shape, dim)
+
+
+def layer_kernel(
+    chips,
+    ids_ref,
+    logits_ref,
+    new_ref,
+    slot_ref,
+    length_ref,
+    hidden_hbm,
+    residual_hbm,
+    queries_hbm,
+    cache_hbm,
+    gate_hbm,
+    up_hbm,
+    down_hbm,
+    mixed_ref,
+    attended_hbm,
+    weights,
+    hidden,
+    residual,
+    queries,
+    cache,
+    attended,
+    visible,
+    order_in,
+    order_out,
+    mix_high,
+    mix_low,
+    staged,
+    arrived,
+    rows,
+    projected,
+    activated,
+    own_part,
+    part_send,
+    part_recv,
+    back_send,
+    back_recv,
+    load_sem,
+    weight_sem,
+    out_sem,
+    give_send,
+    give_recv,
+    pass_send,
+    pass_recv,
+    part_ssem,
+    part_rsem,
+    back_ssem,
+    back_rsem,
+):
+    sec = lax.axis_index("sec")
+    chip = sec // 2
+    core = sec % 2
+    partner = {"sec": chip * 2 + (1 - core)}
+    tokens, width = hidden.shape
+    blocks = width // BLOCK
+    halves = activated.shape[1] // BLOCK
+    sources = 2 * chips
+    items = sources * CAP
+    own_rows = chips * CAP
+    mine = chips * CAP * SUB
+
+    def chip_after(d):
+        return (chip + d) % chips
+
+    def chip_before(d):
+        return (chip + chips - d) % chips
+
+    def peer(d):
+        return {"sec": chip_after(d) * 2 + core}
+
+    barrier = pltpu.get_barrier_semaphore()
+    for d in range(1, chips):
+        pl.semaphore_signal(barrier, inc=1, device_id=peer(d), device_id_type=MESH)
+    pl.semaphore_signal(barrier, inc=1, device_id=partner, device_id_type=MESH)
+
+    loads = [
+        pltpu.make_async_copy(src, dst, load_sem.at[i])
+        for i, (src, dst) in enumerate(
+            ((hidden_hbm, hidden), (queries_hbm, queries), (cache_hbm, cache), (residual_hbm, residual))
+        )
+    ]
+    for load in loads:
+        load.start()
+
+    per = 2 * halves
+
+    def first_tile(j, q, slot):
+        source = gate_hbm if q % 2 == 0 else up_hbm
+        return pltpu.make_async_copy(
+            source.at[pl.ds(pl.multiple_of(j * BLOCK, BLOCK), BLOCK), pl.ds((q // 2) * BLOCK, BLOCK)],
+            weights.at[slot],
+            weight_sem.at[slot],
+        )
+
+    def second_tile(j, h, slot):
+        return pltpu.make_async_copy(
+            down_hbm.at[pl.ds(h * BLOCK, BLOCK), pl.ds(pl.multiple_of(j * BLOCK, BLOCK), BLOCK)],
+            weights.at[slot],
+            weight_sem.at[slot],
+        )
+
+    def fill(j, carry):
+        for q in range(per):
+            first_tile(j, q, per * j + q).start()
+        return carry
+
+    lax.fori_loop(0, SLOTS // per, fill, 0)
+
+    ids = ids_ref[...]
+    raised = jax.nn.sigmoid(logits_ref[...])
+    gate_weight = raised / jnp.sum(raised, axis=1, keepdims=True)
+    column = iota((tokens, mine), 1)
+    expert = column // (CAP * SUB)
+    position = (column // SUB) % CAP
+    named = jnp.zeros((tokens, mine), jnp.float32)
+    weight = jnp.zeros((tokens, mine), jnp.float32)
+    for choice in range(TOP):
+        hit = ids[:, choice : choice + 1] == expert
+        named = named + jnp.where(hit, 1.0, 0.0)
+        weight = weight + jnp.where(hit, gate_weight[:, choice : choice + 1], 0.0)
+    row = iota((tokens, mine), 0)
+    earlier = jnp.zeros((tokens, mine), jnp.float32)
+    for t in range(tokens - 1):
+        earlier = earlier + jnp.where(row > t, named[t : t + 1, :], 0.0)
+    taken = jnp.where(earlier == position.astype(jnp.float32), named, 0.0)
+    weight = weight * taken
+    if tokens < 8:
+        blank = jnp.zeros((8 - tokens, mine), jnp.float32)
+        taken = jnp.concatenate([taken, blank], axis=0)
+        weight = jnp.concatenate([weight, blank], axis=0)
+    piece = iota((8, mine), 1) % SUB
+    select = jnp.concatenate([jnp.where(piece == i, taken, 0.0) for i in range(SUB)], axis=0)
+    mix = jnp.concatenate([jnp.where(piece == i, weight, 0.0) for i in range(SUB)], axis=0)
+    high = mix.astype(jnp.bfloat16)
+    mix_high[...] = high
+    mix_low[...] = (mix - high.astype(jnp.float32)).astype(jnp.bfloat16)
+
+    loads[0].wait()
+    full = hidden[...].astype(jnp.float32)
+    if tokens < 8:
+        full = jnp.concatenate([full, jnp.zeros((8 - tokens, width), jnp.float32)], axis=0)
+    stacked = jnp.concatenate(
+        [
+            jnp.concatenate(
+                [full[:, j * BLOCK + i * LANES : j * BLOCK + (i + 1) * LANES] for j in range(blocks)], axis=1
+            )
+            for i in range(SUB)
+        ],
+        axis=0,
+    ).astype(jnp.bfloat16)
+    packed = lax.dot_general(
+        select.astype(jnp.bfloat16), stacked, (((0,), (0,)), ((), ())), preferred_element_type=jnp.float32
+    )
+    staged[...] = packed.astype(jnp.bfloat16).reshape(staged.shape)
+
+    pl.semaphore_wait(barrier, chips)
+
+    def give(d):
+        return pltpu.make_async_remote_copy(
+            src_ref=staged.at[chip_after(d)],
+            dst_ref=arrived.at[core, chip],
+            send_sem=give_send.at[d],
+            recv_sem=give_recv.at[d],
+            device_id=peer(d),
+            device_id_type=MESH,
+        )
+
+    def hand_over(d):
+        source = staged.at[chip] if d == 0 else arrived.at[core, chip_before(d)]
+        return pltpu.make_async_remote_copy(
+            src_ref=source,
+            dst_ref=arrived.at[core, chip_before(d)],
+            send_sem=pass_send.at[d],
+            recv_sem=pass_recv.at[d],
+            device_id=partner,
+            device_id_type=MESH,
+        )
+
+    for d in range(1, chips):
+        give(d).start()
+    hand_over(0).start()
+    arrived[core, chip] = staged[chip]
+
+    count = items * SUB
+    to, frm = iota((count, count), 0), iota((count, count), 1)
+    wanted = ((to % items) // CAP) * (CAP * SUB) + (to % CAP) * SUB + to // items
+    order_in[...] = jnp.where(frm == wanted, 1.0, 0.0).astype(jnp.bfloat16)
+    to, frm = iota((mine, mine), 0), iota((mine, mine), 1)
+    wanted = (to % SUB) * own_rows + to // SUB
+    order_out[...] = jnp.where(frm == wanted, 1.0, 0.0).astype(jnp.bfloat16)
+
+    requests, held, both = cache.shape
+    head = both // 2
+    heads = queries.shape[1] // head
+    span = requests * held
+    request = iota((requests, span), 0)
+    place = iota((requests, span), 1)
+    slot_of = jnp.zeros((requests, span), jnp.int32)
+    length_of = jnp.zeros((requests, span), jnp.int32)
+    for r in range(requests):
+        slot_of = jnp.where(request == r, slot_ref[0, r], slot_of)
+        length_of = jnp.where(request == r, length_ref[r], length_of)
+    seen = (place // held == slot_of) & (place % held < length_of)
+    visible[...] = jnp.where(seen, 1.0, 0.0)
+    loads[1].wait()
+    loads[2].wait()
+    inverse_root = 1.0 / math.sqrt(head)
+
+    def attend(g, carry):
+        base = pl.multiple_of(g * (HEADS_STEP * head), HEADS_STEP * head)
+        asked = jnp.concatenate(
+            [queries[:, pl.ds(base + h * head, head)].astype(jnp.float32) for h in range(HEADS_STEP)], axis=0
+        )
+        keys = cache[:, :, 0:head].reshape(span, head)
+        values = cache[:, :, head:both].reshape(span, head)
+        new_key = jnp.concatenate([new_ref[:, 0:head].astype(jnp.float32)] * HEADS_STEP, axis=0)
+        new_value = jnp.concatenate([new_ref[:, head:both].astype(jnp.float32)] * HEADS_STEP, axis=0)
+        shown = jnp.concatenate([visible[...]] * HEADS_STEP, axis=0) > 0.5
+        scores = (
+            lax.dot_general(
+                asked.astype(jnp.bfloat16), keys, (((1,), (1,)), ((), ())), preferred_element_type=jnp.float32
+            )
+            * inverse_root
+        )
+        scores = jnp.where(shown, scores, NEG_FILL)
+        own = jnp.sum(asked * new_key, axis=1, keepdims=True) * inverse_root
+        top = jnp.maximum(jnp.max(scores, axis=1, keepdims=True), own)
+        lifted = jnp.where(shown, jnp.exp(scores - top), 0.0)
+        own_lift = jnp.exp(own - top)
+        scale = 1.0 / (jnp.sum(lifted, axis=1, keepdims=True) + own_lift)
+        chances = (lifted * scale).astype(jnp.bfloat16)
+        own_chance = (own_lift * scale).astype(jnp.bfloat16).astype(jnp.float32)
+        result = jnp.dot(chances, values, preferred_element_type=jnp.float32) + own_chance * new_value
+        for h in range(HEADS_STEP):
+            attended[:, pl.ds(base + h * head, head)] = result[h * requests : (h + 1) * requests].astype(
+                jnp.bfloat16
+            )
+        return carry
+
+    steps = heads // HEADS_STEP
+    lax.fori_loop(0, steps // 2, attend, 0)
+    for d in range(1, chips):
+        give(d).wait_recv()
+        hand_over(d).start()
+    lax.fori_loop(steps // 2, steps, attend, 0)
+    finished = pltpu.make_async_copy(attended, attended_hbm, out_sem)
+    finished.start()
+    for d in range(chips):
+        hand_over(d).wait_recv()
+
+    ordered = jnp.dot(
+        order_in[...], arrived[...].reshape(count, blocks * LANES), preferred_element_type=jnp.float32
+    ).astype(jnp.bfloat16)
+    for j in range(blocks):
+        for i in range(SUB):
+            rows[j, :, i * LANES : (i + 1) * LANES] = ordered[
+                i * items : (i + 1) * items, j * LANES : (j + 1) * LANES
+            ]
+
+    projected[...] = jnp.zeros_like(projected)
+
+    def first(j, carry):
+        taken_rows = rows[j]
+        for q in range(per):
+            slot = (per * j + q) % SLOTS
+            first_tile(j, q, slot).wait()
+            projected[q] += jnp.dot(taken_rows, weights[slot], preferred_element_type=jnp.float32)
+            later = j + SLOTS // per
+
+            @pl.when(later < blocks)
+            def _():
+                first_tile(later, q, slot).start()
+
+            tile = per * (later - blocks) + q
+
+            @pl.when((later >= blocks) & (tile < blocks * halves))
+            def _():
+                second_tile(tile // halves, q % halves, slot).start()
+
+        return carry
+
+    lax.fori_loop(0, blocks, first, 0)
+    for h in range(halves):
+        gate_proj, up_proj = projected[2 * h], projected[2 * h + 1]
+        activated[:, h * BLOCK : (h + 1) * BLOCK] = (
+            gate_proj / (1.0 + jnp.exp(-gate_proj)) * up_proj
+        ).astype(jnp.bfloat16)
+
+    def exchange(j):
+        return pltpu.make_async_remote_copy(
+            src_ref=part_send.at[j],
+            dst_ref=part_recv.at[j],
+            send_sem=part_ssem.at[j],
+            recv_sem=part_rsem.at[j],
+            device_id=partner,
+            device_id_type=MESH,
+        )
+
+    def give_back(j, d):
+        return pltpu.make_async_remote_copy(
+            src_ref=back_send.at[j, chip_after(d)],
+            dst_ref=back_recv.at[j, chip],
+            send_sem=back_ssem.at[j, d],
+            recv_sem=back_rsem.at[j, d],
+            device_id=peer(d),
+            device_id_type=MESH,
+        )
+
+    def second(j):
+        total = jnp.zeros((items, BLOCK), jnp.float32)
+        for h in range(halves):
+            slot = (blocks * per + halves * j + h) % SLOTS
+            second_tile(j, h, slot).wait()
+            total = total + jnp.dot(
+                activated[:, h * BLOCK : (h + 1) * BLOCK], weights[slot], preferred_element_type=jnp.float32
+            )
+        here, there = total[0:own_rows], total[own_rows:items]
+        part_send[j] = jnp.where(core == 0, there, here).astype(jnp.bfloat16)
+        own_part[j] = jnp.where(core == 0, here, there)
+        exchange(j).start()
+
+    def send_back(j):
+        exchange(j).wait_recv()
+        summed = (own_part[j] + part_recv[j].astype(jnp.float32)).astype(jnp.bfloat16)
+        pieces = jnp.concatenate([summed[:, i * LANES : (i + 1) * LANES] for i in range(SUB)], axis=0)
+        back_send[j] = (
+            jnp.dot(order_out[...], pieces, preferred_element_type=jnp.float32)
+            .astype(jnp.bfloat16)
+            .reshape(chips, CAP * SUB, LANES)
+        )
+        for d in range(1, chips):
+            give_back(j, d).start()
+        back_recv[j, chip] = back_send[j, chip]
+
+    def combine(j):
+        for d in range(1, chips):
+            give_back(j, d).wait_recv()
+        returned = back_recv[j].reshape(mine, LANES)
+        total = jnp.dot(mix_high[...], returned, preferred_element_type=jnp.float32) + jnp.dot(
+            mix_low[...], returned, preferred_element_type=jnp.float32
+        )
+        base = pl.multiple_of(j * BLOCK, BLOCK)
+        for i in range(SUB):
+            at = pl.ds(base + i * LANES, LANES)
+            mixed_ref[:, at] = (
+                residual[:, at].astype(jnp.float32) + total[i * 8 : i * 8 + tokens]
+            ).astype(jnp.bfloat16)
+
+    loads[3].wait()
+
+    def down(j, carry):
+        second(j)
+
+        @pl.when(j >= 1)
+        def _():
+            send_back(j - 1)
+
+        @pl.when(j >= 2)
+        def _():
+            combine(j - 2)
+
+        return carry
+
+    lax.fori_loop(0, blocks, down, 0)
+    send_back(blocks - 1)
+    combine(blocks - 2)
+    combine(blocks - 1)
+
+    for d in range(1, chips):
+        give(d).wait_send()
+    for d in range(chips):
+        hand_over(d).wait_send()
+
+    def drain(j, carry):
+        exchange(j).wait_send()
+        for d in range(1, chips):
+            give_back(j, d).wait_send()
+        return carry
+
+    lax.fori_loop(0, blocks, drain, 0)
+    finished.wait()
+
+
+def fused_layer(
+    hidden_rows,
+    residual,
+    expert_ids,
+    router_logits,
+    w_gate,
+    w_up,
+    w_down,
+    queries,
+    new_kv,
+    kv_cache,
+    cache_slot,
+    cache_lengths,
+):
+    chips = lax.axis_size("sec") // 2
+    tokens, width = hidden_rows.shape
+    hidden_each = w_gate.shape[1]
+    blocks = width // BLOCK
+    halves = hidden_each // BLOCK
+    requests, held, both = kv_cache.shape
+    items = 2 * chips * CAP
+    mine = chips * CAP * SUB
+    vmem = pl.BlockSpec(memory_space=pltpu.VMEM)
+    smem = pl.BlockSpec(memory_space=pltpu.SMEM)
+    anywhere = pl.BlockSpec(memory_space=pl.ANY)
+    bf16, f32 = jnp.bfloat16, jnp.float32
+    dma = pltpu.SemaphoreType.DMA
+    return pl.pallas_call(
+        functools.partial(layer_kernel, chips),
+        out_shape=(
+            jax.ShapeDtypeStruct((tokens, width), bf16),
+            jax.ShapeDtypeStruct(queries.shape, bf16),
+        ),
+        in_specs=[vmem, vmem, vmem, smem, smem] + [anywhere] * 7,
+        out_specs=(vmem, anywhere),
+        scratch_shapes=[
+            pltpu.VMEM((SLOTS, BLOCK, BLOCK), bf16),
+            pltpu.VMEM((tokens, width), bf16),
+            pltpu.VMEM((tokens, width), bf16),
+            pltpu.VMEM(queries.shape, bf16),
+            pltpu.VMEM(kv_cache.shape, bf16),
+            pltpu.VMEM(queries.shape, bf16),
+            pltpu.VMEM((requests, requests * held), f32),
+            pltpu.VMEM((items * SUB, items * SUB), bf16),
+            pltpu.VMEM((mine, mine), bf16),
+            pltpu.VMEM((8 * SUB, mine), bf16),
+            pltpu.VMEM((8 * SUB, mine), bf16),
+            pltpu.VMEM((chips, CAP * SUB, blocks * LANES), bf16),
+            pltpu.VMEM((2, chips, CAP * SUB, blocks * LANES), bf16),
+            pltpu.VMEM((blocks, items, BLOCK), bf16),
+            pltpu.VMEM((2 * halves, items, BLOCK), f32),
+            pltpu.VMEM((items, hidden_each), bf16),
+            pltpu.VMEM((blocks, chips * CAP, BLOCK), f32),
+            pltpu.VMEM((blocks, chips * CAP, BLOCK), bf16),
+            pltpu.VMEM((blocks, chips * CAP, BLOCK), bf16),
+            pltpu.VMEM((blocks, chips, CAP * SUB, LANES), bf16),
+            pltpu.VMEM((blocks, chips, CAP * SUB, LANES), bf16),
+            dma((4,)),
+            dma((SLOTS,)),
+            dma,
+            dma((chips,)),
+            dma((chips,)),
+            dma((chips,)),
+            dma((chips,)),
+            dma((blocks,)),
+            dma((blocks,)),
+            dma((blocks, chips)),
+            dma((blocks, chips)),
+        ],
+        compiler_params=pltpu.CompilerParams(
+            collective_id=0, has_side_effects=True, vmem_limit_bytes=VMEM_BYTES
+        ),
+        cost_estimate=pl.CostEstimate(
+            flops=6 * items * width * hidden_each,
+            bytes_accessed=6 * width * hidden_each,
+            transcendentals=0,
+        ),
+    )(
+        expert_ids,
+        router_logits,
+        new_kv,
+        cache_slot,
+        cache_lengths,
+        hidden_rows,
+        residual,
+        queries,
+        kv_cache,
+        w_gate,
+        w_up,
+        w_down,
+    )
 
 
 def slot_codes(expert_ids, capacity):
@@ -21,7 +511,7 @@
     return (flattened * capacity + position).reshape(expert_ids.shape)
 
 
-def per_device(
+def plain_layer(
     hidden_rows,
     residual,
     expert_ids,
@@ -110,6 +600,18 @@
     return (mixed, attended)
 
 
+def per_device(hidden_rows, residual, expert_ids, router_logits, w_gate, w_up, w_down, queries, *rest):
+    fits = (
+        lax.axis_size("sec") == 2 * EXPERTS
+        and hidden_rows.shape[0] <= 8
+        and hidden_rows.shape[1] % BLOCK == 0
+        and w_gate.shape[1] == 2 * BLOCK
+        and SLOTS // 4 <= hidden_rows.shape[1] // BLOCK
+    )
+    layer = fused_layer if fits else plain_layer
+    return layer(hidden_rows, residual, expert_ids, router_logits, w_gate, w_up, w_down, queries, *rest)
+
+
 def solution(mesh):
     placed = (
         P(("groups", "sec"), None),

time: 79.8 us -> 54.5 us (0.68)
  Pallas kernels: 0 us -> 50.5 us
  matrix products: 36.6 us -> 0 us
  waiting for transfers between devices: 19.7 us -> 0 us
  starting transfers between devices: 11.3 us -> 0 us
  other arithmetic: 4.97 us -> 0 us
  local copies, waits for them, and re-layouts: 5.89 us -> 3.13 us
    pallas_call x0 -> x1, Pallas kernels: none -> 50.5 us  [fused_layer(): pl.pallas_call(functools.partial(layer_kernel, chips), out_shape=(jax.Sha...]
    dot_general x6 -> x0, matrix products: 36.6 us -> none  [the longest x1 20.8 us: per_device(): jnp.dot(activated, w_down, preferred_element_type=jnp.float32)]
    all_to_all x2 -> x0, waiting for transfers between devices: 19.7 us -> none  [the longest x1 11.6 us: per_device(): lax.all_to_all(partial_value, 'sec', split_axis=0, concat_axis=0, tiled=T...]
    all_to_all x2 -> x0, starting transfers between devices: 11.3 us -> none  [the longest x1 7.39 us: per_device(): lax.all_to_all(outgoing, 'sec', split_axis=0, concat_axis=0, tiled=True)]
    unnamed x7 -> x2, local copies, waits for them, and re-layouts: 0.87 us -> 3.13 us
    reshape x4 -> x0, local copies, waits for them, and re-layouts: 1.59 us -> none  [the longest x1 0.94 us: per_device(): partial_value = partial_value.reshape(devices, items, model_width)]
    reduce_sum x6 -> x0, other arithmetic: 1.26 us -> none  [the longest x1 0.52 us: per_device(): jnp.sum(returned.astype(jnp.float32).reshape(EXPERTS, shards, capacity, m...]
    gather x2 -> x0, local copies, waits for them, and re-layouts: 1.25 us -> none  [the longest x1 0.67 us: per_device(): gathered[coded.reshape(-1)].reshape(tokens_here, TOP, model_width)]
  transfers between devices with their start and end apart: 2 -> 0, of which waited for: 2 -> 0; matrix products, arithmetic and copies ran while one was open for 9% -> 0% of each run, Pallas kernels for 0% -> 0%
where the time goes in v1:
time: 54.5 us; the launch traced here: 54.3 us
  Pallas kernels  50.5 us (93%)
  local copies, waits for them, and re-layouts  3.13 us (6%)
  between operations  0.64 us (1%)
    pallas_call x1, Pallas kernels, fused_layer(): pl.pallas_call(functools.partial(layer_kernel, chips), out_shape=(jax.Sha...  50.5 us
    unnamed x2, local copies, waits for them, and re-layouts  3.13 us

profile of v1, /device:TPU:0, one launch (start us, length us, event | category | flops | bytes accessed | tf_op | source)
XLA Modules:
  0.0 54.3 jit_solution(483438424582105905)
XLA Ops:
  0.6 50.5 %shard_map.131 = (bf16[4,7168]{1,0:T(4,128)(2,1)}, bf16[8,16384]{1,0:T(8,128)(2,1)}) custom-call(s32[4,3]{1,0:T(4,128)} %ids_ref.1, f32[4,3]{1,0:T(4,128)} %logits_ref.1, bf16[8,512]{1,0:T(8,128)(2,1)} %new_ref.1, s32[1,8]{1,0:T(1,128)} %slot_ref.1, s32[8]{0:T(128)} %length_ref.1, bf16[4,7168]{1,0:T(4,128)(2,1)} %hidden_hbm.1, bf16[4,7168]{1,0:T(4,128)(2,1)} %residual_hbm.1, ...), custom_call_target="tpu_custom_call" | custom-call | flops 2818572288 | bytes 88080384 | tf_op jit(solution)/shard_map/pallas_call | solution.py:440
  51.2 1.5 %copy.16 = bf16[4,7168]{1,0:T(4,128)(2,1)} copy(bf16[4,7168]{1,0:T(4,128)(2,1)} %get-tuple-element.4) | data formatting | bytes 114688
  52.6 1.7 %copy.17 = bf16[8,16384]{1,0:T(8,128)(2,1)} copy(bf16[8,16384]{1,0:T(8,128)(2,1)} %get-tuple-element.5) | data formatting | bytes 524288

commit v2 on v1

--- a/solution.py
+++ b/solution.py
@@ -20,6 +20,7 @@
 VMEM_BYTES = 63 * 1024 * 1024
 SLOTS = 28
 HEADS_STEP = 16
+GROUPS = ((0, 3), (3, 5), (5, 7))
 MESH = pl.DeviceIdType.MESH
 
 
@@ -325,12 +326,17 @@
             device_id_type=MESH,
         )
 
-    def give_back(j, d):
+    def lanes(j):
+        return pl.ds(pl.multiple_of(j * LANES, LANES), LANES)
+
+    def give_back(g, d):
+        low, high = GROUPS[g]
+        span = pl.ds(low * LANES, (high - low) * LANES)
         return pltpu.make_async_remote_copy(
-            src_ref=back_send.at[j, chip_after(d)],
-            dst_ref=back_recv.at[j, chip],
-            send_sem=back_ssem.at[j, d],
-            recv_sem=back_rsem.at[j, d],
+            src_ref=back_send.at[chip_after(d), :, span],
+            dst_ref=back_recv.at[chip, :, span],
+            send_sem=back_ssem.at[g, d],
+            recv_sem=back_rsem.at[g, d],
             device_id=peer(d),
             device_id_type=MESH,
         )
@@ -352,19 +358,21 @@
         exchange(j).wait_recv()
         summed = (own_part[j] + part_recv[j].astype(jnp.float32)).astype(jnp.bfloat16)
         pieces = jnp.concatenate([summed[:, i * LANES : (i + 1) * LANES] for i in range(SUB)], axis=0)
-        back_send[j] = (
+        back_send[:, :, lanes(j)] = (
             jnp.dot(order_out[...], pieces, preferred_element_type=jnp.float32)
             .astype(jnp.bfloat16)
             .reshape(chips, CAP * SUB, LANES)
         )
-        for d in range(1, chips):
-            give_back(j, d).start()
-        back_recv[j, chip] = back_send[j, chip]
+        back_recv[chip, :, lanes(j)] = back_send[chip, :, lanes(j)]
+        for g, (low, high) in enumerate(GROUPS):
+
+            @pl.when(j == high - 1)
+            def _():
+                for d in range(1, chips):
+                    give_back(g, d).start()
 
     def combine(j):
-        for d in range(1, chips):
-            give_back(j, d).wait_recv()
-        returned = back_recv[j].reshape(mine, LANES)
+        returned = back_recv[:, :, lanes(j)].reshape(mine, LANES)
         total = jnp.dot(mix_high[...], returned, preferred_element_type=jnp.float32) + jnp.dot(
             mix_low[...], returned, preferred_element_type=jnp.float32
         )
@@ -384,16 +392,15 @@
         def _():
             send_back(j - 1)
 
-        @pl.when(j >= 2)
-        def _():
-            combine(j - 2)
-
         return carry
 
     lax.fori_loop(0, blocks, down, 0)
-    send_back(blocks - 1)
-    combine(blocks - 2)
-    combine(blocks - 1)
+    send_back(jnp.int32(blocks - 1))
+    for g, (low, high) in enumerate(GROUPS):
+        for d in range(1, chips):
+            give_back(g, d).wait_recv()
+        for j in range(low, high):
+            combine(jnp.int32(j))
 
     for d in range(1, chips):
         give(d).wait_send()
@@ -402,11 +409,12 @@
 
     def drain(j, carry):
         exchange(j).wait_send()
+        return carry
+
+    lax.fori_loop(0, blocks, drain, 0)
+    for g in range(len(GROUPS)):
         for d in range(1, chips):
-            give_back(j, d).wait_send()
-        return carry
-
-    lax.fori_loop(0, blocks, drain, 0)
+            give_back(g, d).wait_send()
     finished.wait()
 
 
@@ -465,8 +473,8 @@
             pltpu.VMEM((blocks, chips * CAP, BLOCK), f32),
             pltpu.VMEM((blocks, chips * CAP, BLOCK), bf16),
             pltpu.VMEM((blocks, chips * CAP, BLOCK), bf16),
-            pltpu.VMEM((blocks, chips, CAP * SUB, LANES), bf16),
-            pltpu.VMEM((blocks, chips, CAP * SUB, LANES), bf16),
+            pltpu.VMEM((chips, CAP * SUB, blocks * LANES), bf16),
+            pltpu.VMEM((chips, CAP * SUB, blocks * LANES), bf16),
             dma((4,)),
             dma((SLOTS,)),
             dma,
@@ -476,8 +484,8 @@
             dma((chips,)),
             dma((blocks,)),
             dma((blocks,)),
-            dma((blocks, chips)),
-            dma((blocks, chips)),
+            dma((len(GROUPS), chips)),
+            dma((len(GROUPS), chips)),
         ],
         compiler_params=pltpu.CompilerParams(
             collective_id=0, has_side_effects=True, vmem_limit_bytes=VMEM_BYTES
@@ -606,6 +614,7 @@
         and hidden_rows.shape[0] <= 8
         and hidden_rows.shape[1] % BLOCK == 0
         and w_gate.shape[1] == 2 * BLOCK
+        and hidden_rows.shape[1] // BLOCK == GROUPS[-1][1]
         and SLOTS // 4 <= hidden_rows.shape[1] // BLOCK
     )
     layer = fused_layer if fits else plain_layer

time: 54.5 us -> 47.1 us (0.86)
  Pallas kernels: 50.5 us -> 43.1 us
    pallas_call x1, Pallas kernels: 50.5 us -> 43.1 us  [fused_layer(): pl.pallas_call(functools.partial(layer_kernel, chips), out_shape=(jax.Sha...]
where the time goes in v2:
time: 47.1 us; the launch traced here: 46.9 us
  Pallas kernels  43.1 us (92%)
  local copies, waits for them, and re-layouts  3.13 us (7%)
  between operations  0.64 us (1%)
    pallas_call x1, Pallas kernels, fused_layer(): pl.pallas_call(functools.partial(layer_kernel, chips), out_shape=(jax.Sha...  43.1 us
    unnamed x2, local copies, waits for them, and re-layouts  3.13 us

profile of v2, /device:TPU:0, one launch (start us, length us, event | category | flops | bytes accessed | tf_op | source)
XLA Modules:
  0.0 46.9 jit_solution(4074348803403063793)
XLA Ops:
  0.6 43.1 %shard_map.131 = (bf16[4,7168]{1,0:T(4,128)(2,1)}, bf16[8,16384]{1,0:T(8,128)(2,1)}) custom-call(s32[4,3]{1,0:T(4,128)} %ids_ref.1, f32[4,3]{1,0:T(4,128)} %logits_ref.1, bf16[8,512]{1,0:T(8,128)(2,1)} %new_ref.1, s32[1,8]{1,0:T(1,128)} %slot_ref.1, s32[8]{0:T(128)} %length_ref.1, bf16[4,7168]{1,0:T(4,128)(2,1)} %hidden_hbm.1, bf16[4,7168]{1,0:T(4,128)(2,1)} %residual_hbm.1, ...), custom_call_target="tpu_custom_call" | custom-call | flops 2818572288 | bytes 88080384 | tf_op jit(solution)/shard_map/pallas_call | solution.py:448
  43.7 1.5 %copy.16 = bf16[4,7168]{1,0:T(4,128)(2,1)} copy(bf16[4,7168]{1,0:T(4,128)(2,1)} %get-tuple-element.4) | data formatting | bytes 114688
  45.2 1.7 %copy.17 = bf16[8,16384]{1,0:T(8,128)(2,1)} copy(bf16[8,16384]{1,0:T(8,128)(2,1)} %get-tuple-element.5) | data formatting | bytes 524288
